TPU v7x, 32 devices: a whole 2x2x4 slice. The times are simulated.
32 devices in a mesh: chan: 8 (over z, x), tm: 4 (over y, core).
Axes of the slice: x: 2, y: 2, z: 4, core: 2. Of those that a mesh axis runs over, the one named last changes fastest.
Arguments:
- traces: bfloat16 [32, 2048, 256], P('tm', 'chan')
- tile_list: int32 [8, 2], P('chan'), may hold values from 0 to 7, as said below
- seg_counts: int32 [8], P('chan'), may hold values from 0 to 32, as said below
Outputs:
- correlations: bfloat16 [8, 256, 256, 128], P('chan', 'tm')
Inputs may be any that keep to these rules, and one draw needn't show every extreme that they name: `tile_list`: for a slot of chan index c, the row block lies within c - 1 .. c + 1 and the column block lies within row block .. row block + 1 and within c - 1 .. c + 1; both are valid block numbers, and 0 and 7 are both used. `seg_counts`: A count of 0 marks an empty slot; both ends are reached.
All inputs are finite; a program needn't handle non-finite values.
Results may differ from a plain program's by a relative error of at most 0.0076.
Values may be sent and summed in bfloat16 or wider, within the bound.
A program may use at most 128 MiB of HBM per device.

v0:
```python
import math

import jax
import jax.numpy as jnp
from jax import lax
from jax.sharding import PartitionSpec as P

NF = 128
LAGS = 128


def shifted(block, axis, distance):
    devices = range(lax.axis_size(axis))
    route = [(i - distance, i) for i in devices if i - distance in devices]
    return lax.ppermute(block, axis, route)


def forward_table(samples, nbins):
    n_idx = jnp.arange(samples, dtype=jnp.int32)[:, None]
    k_idx = jnp.arange(1, nbins + 1, dtype=jnp.int32)[None, :]
    phase = (n_idx * k_idx % samples).astype(jnp.float32) * (2.0 * math.pi / samples)
    return jnp.concatenate([jnp.cos(phase), -jnp.sin(phase)], axis=1).astype(jnp.bfloat16)


def inverse_table(samples, nbins, nlags):
    k_idx = jnp.arange(1, nbins + 1, dtype=jnp.int32)[:, None]
    lag_idx = jnp.arange(nlags, dtype=jnp.int32)[None, :] - nlags // 2
    phase = (k_idx * lag_idx % samples).astype(jnp.float32) * (2.0 * math.pi / samples)
    norm = 1.0 / math.sqrt(nbins)
    return (jnp.concatenate([jnp.cos(phase), -jnp.sin(phase)], axis=0) * norm).astype(jnp.bfloat16)


def body(traces, tile_list, seg_counts):
    seg_here, block, samples = traces.shape
    nbins = NF
    spectra = jnp.dot(
        traces.reshape(-1, samples),
        forward_table(samples, nbins),
        preferred_element_type=jnp.float32,
    )
    spectra = spectra.reshape(seg_here, block, 2 * nbins)
    energy = lax.psum(jnp.sum(spectra * spectra, axis=(0, 2)), "tm")
    nseg = seg_here * lax.axis_size("tm")
    scale = 1.0 / jnp.sqrt(energy / (nseg * nbins) + 1e-06)
    white = (spectra * scale[None, :, None]).astype(jnp.bfloat16)
    every_seg = lax.all_gather(white, "tm", axis=0, tiled=True)
    beside = {}
    for offset in (1, -1):
        beside[offset] = shifted(every_seg, "chan", offset)
    window = jnp.stack([beside[1], every_seg, beside[-1]], axis=0)
    itable = inverse_table(samples, nbins, LAGS)
    centre = lax.axis_index("chan")
    quarter = block // lax.axis_size("tm")
    row_start = lax.axis_index("tm") * quarter
    seg_ids = jnp.arange(nseg, dtype=jnp.int32)

    def one_slot(slot):
        row_b = tile_list[slot, 0] - centre + 1
        col_b = tile_list[slot, 1] - centre + 1
        count = seg_counts[slot]
        left = lax.dynamic_index_in_dim(window, row_b, 0, keepdims=False)
        left = lax.dynamic_slice_in_dim(left, row_start, quarter, 1)
        right = lax.dynamic_index_in_dim(window, col_b, 0, keepdims=False)
        live = (seg_ids < count).astype(jnp.bfloat16)
        left = left * live[:, None, None]
        left_pair = jnp.concatenate([left[..., :nbins], left[..., nbins:]], axis=0)
        right_re = jnp.concatenate([right[..., :nbins], right[..., nbins:]], axis=0)
        right_im = jnp.concatenate([right[..., nbins:], -right[..., :nbins]], axis=0)
        real = jnp.einsum("sif,sjf->ijf", left_pair, right_re, preferred_element_type=jnp.float32)
        imag = jnp.einsum("sif,sjf->ijf", left_pair, right_im, preferred_element_type=jnp.float32)
        denom = jnp.maximum(count, 1).astype(jnp.float32)
        cross = (jnp.concatenate([real, imag], axis=-1) / denom).astype(jnp.bfloat16)
        corr = jnp.dot(cross.reshape(-1, 2 * nbins), itable, preferred_element_type=jnp.float32)
        return corr.reshape(quarter, block, LAGS).astype(jnp.bfloat16)

    return lax.map(one_slot, jnp.arange(tile_list.shape[0], dtype=jnp.int32))


def solution(mesh):
    return jax.shard_map(
        body,
        mesh=mesh,
        in_specs=(P("tm", "chan", None), P("chan", None), P("chan")),
        out_specs=P("chan", "tm", None, None),
        check_vma=False,
    )
```

profile of v0, /device:TPU:9, one launch (start us, length us, event | category | flops | bytes accessed | tf_op | source)
XLA Modules:
  0.0 292.9 jit_solution(3167506098277517931)
XLA Ops:
  6.5 0.0 copy-start
  6.5 0.0 all-gather.2.cloned.1.call-start
  6.5 0.6 cosine_convert_fusion
  7.1 0.7 copy-done
  7.8 0.5 fusion.14
  8.3 0.0 copy-start.3
  8.3 0.9 copy.6
  9.2 5.7 %psum.7 = f32[256]{0:T(256)S(1)} all-reduce(f32[256]{0:T(256)S(1)} %reduce_sum.18), channel_id=1, replica_groups=mesh['chan'=8,'tm'=4] {'tm'}, use_global_device_ids=true, to_apply=%region_2.3 | all-reduce | flops 256 | bytes 2048 | tf_op jit(solution)/shard_map/psum | solution.py:42
  14.9 1.1 fusion.13
  16.0 0.0 all-gather.2.cloned.1.call-update
  16.1 37.0 %all-gather.2.cloned.1.call-done = bf16[32,256,256]{1,0,2:T(8,128)(2,1)} async-done(((bf16[8,256,256]{1,0,2:T(8,128)(2,1)}), bf16[32,256,256]{1,0,2:T(8,128)(2,1)}) %all-gather.2.cloned.1.call-update) | async-done | bytes 4194320 | tf_op jit(solution)/shard_map/all_gather | solution.py:46
  53.1 3.1 %collective-permute-start = (bf16[32,256,256]{1,0,2:T(8,128)(2,1)}, bf16[32,256,256]{1,0,2:T(8,128)(2,1)}, u32[]{:S(2)}, u32[]{:S(2)}) collective-permute-start(bf16[32,256,256]{1,0,2:T(8,128)(2,1)} %all-gather.2.cloned.1.call-done), channel_id=1, source_target_pairs={{0,4},{4,8},{8,12},{12,16},{16,20},{20,24},{24,28},{1,5},{5,9},{9,... | collective-permute-start | bytes 12582920 | tf_op jit(solution)/shard_map/ppermute | solution.py:15
  56.2 3.1 %collective-permute-start.1 = (bf16[32,256,256]{1,0,2:T(8,128)(2,1)}, bf16[32,256,256]{1,0,2:T(8,128)(2,1)}, u32[]{:S(2)}, u32[]{:S(2)}) collective-permute-start(bf16[32,256,256]{1,0,2:T(8,128)(2,1)} %all-gather.2.cloned.1.call-done), channel_id=1, source_target_pairs={{4,0},{8,4},{12,8},{16,12},{20,16},{24,20},{28,24},{5,1},{9,5},{13... | collective-permute-start | bytes 12582920 | tf_op jit(solution)/shard_map/ppermute | solution.py:15
  59.3 0.0 copy-done.3
  59.3 0.6 fusion.40
  61.9 0.3 fusion.32
  62.2 173.9 %collective-permute-done = bf16[32,256,256]{1,0,2:T(8,128)(2,1)} collective-permute-done((bf16[32,256,256]{1,0,2:T(8,128)(2,1)}, bf16[32,256,256]{1,0,2:T(8,128)(2,1)}, u32[]{:S(2)}, u32[]{:S(2)}) %collective-permute-start) | collective-permute-done | bytes 4194336 | tf_op jit(solution)/shard_map/ppermute | solution.py:15
  236.1 2.5 collective-permute-done.1
  238.6 6.2 %pad_maximum_fusion = bf16[3,32,256,256]{2,1,3,0:T(8,128)(2,1)S(1)} fusion(bf16[1,32,256,256]{2,1,3,0:T(8,128)(2,1)} %bitcast.4, bf16[1,32,256,256]{2,1,3,0:T(8,128)(2,1)} %bitcast.36, bf16[1,32,256,256]{2,1,3,0:T(8,128)(2,1)} %bitcast.2), kind=kLoop, calls=%fused_computation.2 | loop fusion | flops 12582912 | bytes 25165824 | tf_op jit(solution)/shard_map/stack | solution.py:50
  244.8 0.9 bitcast_multiply_fusion.1
  245.7 0.4 fusion.39
  246.1 0.0 copy-start.2
  246.1 0.5 dynamic-slice_bitcast_fusion
  246.6 1.7 fusion.38
  248.3 0.0 copy-done.2
  248.3 4.0 %fusion.3 = f32[128,256,64]{1,2,0:T(8,128)} fusion(bf16[32,256,128]{1,0,2:T(8,128)(2,1)S(1)} %get-tuple-element.23, bf16[32,256,128]{1,0,2:T(8,128)(2,1)S(1)} %get-tuple-element.21, bf16[32,64,128]{1,0,2:T(8,128)(2,1)S(1)} %get-tuple-element.25, bf16[32,64,128]{1,0,2:T(8,128)(2,1)S(1)} %get-tuple-element.24), kind=kOutput, calls=%fused_computation.4 | convolution fusion | flops 278921216 | bytes 13631488 | tf_op jit(solution)/shard_map/while/body/eval_jaxpr/sif,sjf->ijf/dot_general | solution.py:69
  252.3 9.3 %copy.4 = f32[128,256,64]{0,1,2:T(8,128)} copy(f32[128,256,64]{1,2,0:T(8,128)} %fusion.3) | data formatting | bytes 16777216 | tf_op jit(solution)/shard_map/while/body/eval_jaxpr/sif,sjf->ijf/dot_general | solution.py:69
  261.6 6.4 %fusion.7 = f32[128,256,64]{1,2,0:T(8,128)} fusion(bf16[32,256,128]{1,0,2:T(8,128)(2,1)} %get-tuple-element.22, bf16[32,256,128]{1,0,2:T(8,128)(2,1)S(1)} %get-tuple-element.23, bf16[32,64,128]{1,0,2:T(8,128)(2,1)} %copy-done.2, bf16[32,64,128]{1,0,2:T(8,128)(2,1)S(1)} %get-tuple-element.24), kind=kOutput, calls=%fused_computation.8 | convolution fusion | flops 278921216 | bytes 13631488 | tf_op jit(solution)/shard_map/while/body/eval_jaxpr/sif,sjf->ijf/dot_general | solution.py:70
  267.9 9.3 %copy.5 = f32[128,256,64]{0,1,2:T(8,128)} copy(f32[128,256,64]{1,2,0:T(8,128)} %fusion.7) | data formatting | bytes 16777216 | tf_op jit(solution)/shard_map/while/body/eval_jaxpr/sif,sjf->ijf/dot_general | solution.py:70
  277.2 0.0 copy-start.1
  277.2 8.8 %convert_bitcast_fusion = bf16[1,64,256,128]{3,2,1,0:T(8,128)(2,1)} fusion(f32[64,256,128]{2,1,0:T(8,128)} %bitcast.34, f32[64,256,128]{2,1,0:T(8,128)} %bitcast.33, f32[]{:T(128)S(6)} %convert_element_type.42, f32[128,128]{1,0:T(8,128)S(1)} %get-tuple-element.36, f32[128,128]{1,0:T(8,128)S(1)} %get-tuple-element.26), kind=kOutput, calls=%fused_computation.12 | convolution fusion | flops 1088520192 | bytes 21102596 | tf_op jit(solution)/shard_map/while/body/eval_jaxpr/dot_general | solution.py:73
  286.0 0.0 copy-done.1
  (5 shorter events, 0.0 us)
Async XLA Ops:
  6.5 1.2 copy-start
  6.5 46.6 %all-gather.2.cloned.1.call-start = ((), (), s32[]{:S(2)}) async-start(), calls=%async_computation | async-start | bytes 5242880 | tf_op jit(solution)/shard_map/all_gather | solution.py:46
  8.3 51.0 %copy-start.3 = (s32[1,2]{1,0:T(1,128)S(1)}, s32[1,2]{1,0:T(1,128)}, u32[]{:S(2)}) copy-start(s32[1,2]{1,0:T(1,128)} %param.4) | copy-start | bytes 28
  53.1 183.0 %collective-permute-start = (bf16[32,256,256]{1,0,2:T(8,128)(2,1)}, bf16[32,256,256]{1,0,2:T(8,128)(2,1)}, u32[]{:S(2)}, u32[]{:S(2)}) collective-permute-start(bf16[32,256,256]{1,0,2:T(8,128)(2,1)} %all-gather.2.cloned.1.call-done), channel_id=1, source_target_pairs={{0,4},{4,8},{8,12},{12,16},{16,20},{20,24},{24,28},{1,5},{5,9},{9,... | collective-permute-start | bytes 12582920 | tf_op jit(solution)/shard_map/ppermute | solution.py:15
  56.2 182.4 %collective-permute-start.1 = (bf16[32,256,256]{1,0,2:T(8,128)(2,1)}, bf16[32,256,256]{1,0,2:T(8,128)(2,1)}, u32[]{:S(2)}, u32[]{:S(2)}) collective-permute-start(bf16[32,256,256]{1,0,2:T(8,128)(2,1)} %all-gather.2.cloned.1.call-done), channel_id=1, source_target_pairs={{4,0},{8,4},{12,8},{16,12},{20,16},{24,20},{28,24},{5,1},{9,5},{13... | collective-permute-start | bytes 12582920 | tf_op jit(solution)/shard_map/ppermute | solution.py:15
  246.1 2.2 copy-start.2
  277.2 8.8 %copy-start.1 = (bf16[8,256,256]{2,1,0:T(8,128)(2,1)S(1)}, bf16[8,256,256]{2,1,0:T(8,128)(2,1)}, u32[]{:S(2)}) copy-start(bf16[8,256,256]{2,1,0:T(8,128)(2,1)} %param.3) | copy-start | bytes 3145732
Sparse Core Ops, SparseCore 0:
  16.2 36.8 all-gather.1
where the time goes:
time: 293 us
  waiting for transfers between devices  213 us (73%)
  local copies, waits for them, and re-layouts  21.5 us (7%)
  matrix products  19.7 us (7%)
  between operations  15.5 us (5%)
  other arithmetic  10.9 us (4%)
  starting transfers between devices  6.17 us (2%)
  blocking collectives  5.69 us (2%)
    ppermute x2, waiting for transfers between devices, shifted(): return lax.ppermute(block, axis, route)  176 us
    all_gather x1, waiting for transfers between devices, body(): every_seg = lax.all_gather(white, 'tm', axis=0, tiled=True)  37 us
    dot_general x1, local copies, waits for them, and re-layouts, one_slot(): jnp.einsum('sif,sjf->ijf', left_pair, right_re, preferred_element_type=jn...  9.26 us
    dot_general x1, local copies, waits for them, and re-layouts, one_slot(): jnp.einsum('sif,sjf->ijf', left_pair, right_im, preferred_element_type=jn...  9.26 us
    dot_general x1, matrix products, one_slot(): jnp.dot(cross.reshape(-1, 2 * nbins), itable, preferred_element_type=jnp....  8.84 us
    dot_general x1, matrix products, one_slot(): jnp.einsum('sif,sjf->ijf', left_pair, right_im, preferred_element_type=jn...  6.38 us
    another operation x1, other arithmetic, body(): window = jnp.stack([beside[1], every_seg, beside[-1]], axis=0)  6.22 us
    ppermute x2, starting transfers between devices, shifted(): return lax.ppermute(block, axis, route)  6.17 us
  transfers between devices with their start and end apart: 3, of which 3 were waited for; matrix products, arithmetic and copies ran while one was open for 0% of the time, Pallas kernels for 0%

commit v1 on v0

v1 whole, which is shorter than its diff:
```python
import functools
import math

import jax
import jax.numpy as jnp
from jax import lax
from jax.experimental import pallas as pl
from jax.experimental.pallas import tpu as pltpu
from jax.sharding import PartitionSpec as P

NF = 128
LAGS = 128
LANES = 128
MESH = pl.DeviceIdType.MESH
F32 = jnp.float32
BF16 = jnp.bfloat16


def forward_table(samples, nbins):
    n_idx = jnp.arange(samples, dtype=jnp.int32)[None, :]
    k_idx = jnp.arange(1, nbins + 1, dtype=jnp.int32)[:, None]
    phase = (n_idx * k_idx % samples).astype(F32) * (2.0 * math.pi / samples)
    return jnp.concatenate([jnp.cos(phase), -jnp.sin(phase)], axis=0).astype(BF16)


def inverse_table(samples, nbins, nlags):
    k_idx = jnp.arange(1, nbins + 1, dtype=jnp.int32)[None, :]
    lag_idx = jnp.arange(nlags, dtype=jnp.int32)[:, None] - nlags // 2
    phase = (k_idx * lag_idx % samples).astype(F32) * (2.0 * math.pi / samples)
    norm = 1.0 / math.sqrt(nbins)
    return (jnp.concatenate([jnp.cos(phase), -jnp.sin(phase)], axis=1) * norm).astype(BF16)


def pick(flag, yes, no):
    return jnp.where(flag > 0, yes.astype(F32), no.astype(F32)).astype(BF16)


def exchange(nchan, x_ref, flag_ref, r_ref, l_ref, far, near, got, lsend, wish,
             a_send, a_recv, b_send, b_recv, w_send, w_recv,
             r_send, r_recv, l_send, l_recv):
    segs, block, samples = x_ref.shape
    rows = block // 4
    c = lax.axis_index("chan")
    t = lax.axis_index("tm")
    odd = lax.rem(c, 2)
    partner = c + 1 - 2 * odd
    z_to = lax.rem(c + nchan - 2 + 4 * odd, nchan)
    z_from = lax.rem(c + nchan + 2 - 4 * odd, nchan)
    core = lax.rem(t, 2)
    t1 = t + 1 - 2 * core
    t2 = lax.rem(t + 2, 4)
    t3 = lax.rem(t1 + 2, 4)

    barrier = pltpu.get_barrier_semaphore()
    for where in ((z_to, t), (z_from, t), (partner, t), (c, t1), (c, t2), (c, t3)):
        pl.semaphore_signal(barrier, inc=1, device_id=where, device_id_type=MESH)
    pl.semaphore_wait(barrier, 6)

    def send(src, dst, ss, rs, where):
        return pltpu.make_async_remote_copy(
            src_ref=src, dst_ref=dst, send_sem=ss, recv_sem=rs,
            device_id=where, device_id_type=MESH)

    ask = send(flag_ref.at[pl.ds(0, 8)], wish, w_send, w_recv, (partner, t))
    ask.start()
    hop_a = [send(x_ref.at[k], far.at[k], a_send.at[k], a_recv.at[k], (z_to, t))
             for k in range(segs)]
    hop_b = [send(near.at[k], got.at[k], b_send.at[k], b_recv.at[k], (partner, t))
             for k in range(segs)]

    def share(k, slot, which, where):
        ref = r_ref.at[slot * segs + k]
        return send(ref, ref, r_send.at[which, k], r_recv.at[which, k], where)

    def share_l(k, which, peer):
        return send(lsend.at[k, pl.ds(pl.multiple_of(peer * rows, rows), rows)],
                    l_ref.at[t * segs + k],
                    l_send.at[which, k], l_recv.at[which, k], (c, peer))

    to_y = [share(k, t, 0, (c, t2)) for k in range(segs)]
    to_core = [share(k, t, 1, (c, t1)) for k in range(segs)]
    forward = [share(k, t2, 2, (c, t1)) for k in range(segs)]
    parts = [[share_l(k, w, p) for w, p in enumerate((t2, t3, t1))] for k in range(segs)]

    for k in range(segs):
        hop_a[k].start()
    ask.wait_recv()
    for step in range(segs + 2):
        k = step
        if k < segs:
            hop_a[k].wait_recv()
            near[k] = pick(wish[0:1, :], far[k], x_ref[k])
            hop_b[k].start()
        k = step - 1
        if 0 <= k < segs:
            hop_b[k].wait_recv()
            r_ref[t * segs + k] = pick(flag_ref[8:9, :], got[k], x_ref[k])
            to_y[k].start()
            lsend[k] = pick(flag_ref[16:17, :], got[k], x_ref[k])
            for copy in parts[k]:
                copy.start()
            to_core[k].start()
            l_ref[t * segs + k] = lsend[k, pl.ds(pl.multiple_of(t * rows, rows), rows)]
        k = step - 2
        if 0 <= k < segs:
            to_y[k].wait_recv()
            forward[k].start()
    ask.wait_send()
    for k in range(segs):
        hop_a[k].wait_send()
        hop_b[k].wait_send()
        to_y[k].wait_send()
        to_core[k].wait()
        forward[k].wait()
        for copy in parts[k]:
            copy.wait()


def correlate(count_ref, r_ref, l_ref, fwd_ref, inv_ref, o_ref, rspec, lspec, cross):
    nseg, block, samples = r_ref.shape
    rows = l_ref.shape[1]
    bins = 2 * NF
    nt = (((1,), (1,)), ((), ()))
    count = count_ref[0]
    lane = lax.broadcasted_iota(jnp.int32, (1, 2 * rows), 1)
    halves = block // LANES
    span = nseg * bins
    depth = NF * 2 * rows

    def spectra(s, carry):
        re, le = carry
        fwd = fwd_ref[...]
        spec = lax.dot_general(fwd, r_ref[s], nt, preferred_element_type=F32)
        base = pl.multiple_of(s * bins, bins)
        for h in range(halves):
            rspec[pl.ds(h * span + base, bins), :] = spec[:, h * LANES:(h + 1) * LANES]
        re = re + jnp.sum((spec * spec).reshape(bins // 8, 8, block), axis=0)
        left = l_ref[s]
        both = jnp.concatenate([left, left], axis=0)
        spec = lax.dot_general(fwd, both, nt, preferred_element_type=F32)
        le = le + jnp.sum((spec * spec).reshape(bins // 8, 8, 2 * rows), axis=0)
        top, bottom = spec[:NF], spec[NF:]
        lspec[pl.ds(base, NF), :] = jnp.where(lane < rows, top, -bottom)
        lspec[pl.ds(base + NF, NF), :] = jnp.where(lane < rows, bottom, top)
        return re, le

    re, le = lax.fori_loop(
        0, nseg, spectra,
        (jnp.zeros((8, block), F32), jnp.zeros((8, 2 * rows), F32)))
    rscale = 1.0 / jnp.sqrt(jnp.sum(re, axis=0, keepdims=True) / (nseg * NF) + 1e-06)
    lscale = 1.0 / jnp.sqrt(jnp.sum(le, axis=0, keepdims=True) / (nseg * NF) + 1e-06)
    seg_of = lax.broadcasted_iota(jnp.int32, (2 * nseg, 2 * rows), 0) // 2
    lscale = jnp.where(seg_of < count, jnp.broadcast_to(lscale, (2 * nseg, 2 * rows)), 0.0)

    def one_bin(f, _):
        right = jnp.concatenate(
            [rspec[pl.ds(h * span + f, 2 * nseg, stride=NF), :] for h in range(halves)], axis=1)
        right = (right * rscale).astype(BF16)
        left = (lspec[pl.ds(f, 2 * nseg, stride=NF), :] * lscale).astype(BF16)
        both = lax.dot_general(
            left, right, (((0,), (0,)), ((), ())), preferred_element_type=F32)
        base = pl.multiple_of(f * 2 * rows, 2 * rows)
        for h in range(halves):
            cross[pl.ds(h * depth + base, 2 * rows), :] = both[:, h * LANES:(h + 1) * LANES]
        return 0

    lax.fori_loop(0, NF, one_bin, 0, unroll=4)
    share = 1.0 / jnp.maximum(count, 1).astype(F32)

    def one_row(i, _):
        for h in range(halves):
            real = cross[pl.ds(h * depth + i, NF, stride=2 * rows), :].astype(BF16)
            imag = cross[pl.ds(h * depth + rows + i, NF, stride=2 * rows), :].astype(BF16)
            both = jnp.concatenate([real, imag], axis=0)
            corr = jnp.dot(inv_ref[...], both, preferred_element_type=F32) * share
            o_ref[i, pl.ds(h * LANES, LANES), :] = corr.T.astype(BF16)
        return 0

    lax.fori_loop(0, rows, one_row, 0, unroll=2)


def body(nchan, traces, tile_list, seg_counts):
    segs, block, samples = traces.shape
    ntm = 4
    nseg = segs * ntm
    rows = block // ntm
    c = lax.axis_index("chan")
    row_b, col_b = tile_list[0, 0], tile_list[0, 1]
    beyond = jnp.where(c % 2 == 1, jnp.maximum(row_b, col_b) == c + 1,
                       jnp.minimum(row_b, col_b) == c - 1)
    flags = jnp.stack([beyond, col_b != c, row_b != c]).astype(jnp.int32)
    flags = jnp.broadcast_to(flags[:, None, None], (3, 8, samples)).reshape(24, samples)
    vmem = pl.BlockSpec(memory_space=pltpu.VMEM)
    dma = pltpu.SemaphoreType.DMA
    right, left = pl.pallas_call(
        functools.partial(exchange, nchan),
        out_shape=(jax.ShapeDtypeStruct((nseg, block, samples), BF16),
                   jax.ShapeDtypeStruct((nseg, rows, samples), BF16)),
        in_specs=[vmem, vmem],
        out_specs=(vmem, vmem),
        scratch_shapes=[pltpu.VMEM((segs, block, samples), BF16)] * 4 + [
            pltpu.VMEM((8, samples), jnp.int32),
            dma((segs,)), dma((segs,)), dma((segs,)), dma((segs,)), dma, dma,
            dma((3, segs)), dma((3, segs)), dma((3, segs)), dma((3, segs))],
        compiler_params=pltpu.CompilerParams(
            collective_id=0, has_side_effects=True, vmem_limit_bytes=32 << 20),
        name="exchange",
    )(traces, flags)
    out = pl.pallas_call(
        correlate,
        out_shape=jax.ShapeDtypeStruct((rows, block, LAGS), BF16),
        in_specs=[pl.BlockSpec(memory_space=pltpu.SMEM), vmem, vmem, vmem, vmem],
        out_specs=vmem,
        scratch_shapes=[pltpu.VMEM((block // LANES * nseg * 2 * NF, LANES), F32),
                        pltpu.VMEM((nseg * 2 * NF, 2 * rows), F32),
                        pltpu.VMEM((block // LANES * NF * 2 * rows, LANES), F32)],
        compiler_params=pltpu.CompilerParams(vmem_limit_bytes=56 << 20),
        name="correlate",
    )(seg_counts, right, left, forward_table(samples, NF), inverse_table(samples, NF, LAGS))
    return out[None]


def solution(mesh):
    return jax.shard_map(
        functools.partial(body, mesh.shape["chan"]),
        mesh=mesh,
        in_specs=(P("tm", "chan", None), P("chan", None), P("chan")),
        out_specs=P("chan", "tm", None, None),
        check_vma=False,
    )
```

time: 293 us -> 113 us (0.39)
  waiting for transfers between devices: 213 us -> 0 us
  Pallas kernels: 0 us -> 99.8 us
  matrix products: 19.7 us -> 0 us
  local copies, waits for them, and re-layouts: 21.5 us -> 5.66 us
  between operations: 15.5 us -> 4.32 us
  other arithmetic: 10.9 us -> 2.34 us
  starting transfers between devices: 6.17 us -> 0 us
  blocking collectives: 5.69 us -> 0 us
    ppermute x2 -> x0, waiting for transfers between devices: 176 us -> none  [shifted(): return lax.ppermute(block, axis, route)]
    pallas_call x0 -> x2, Pallas kernels: none -> 99.8 us  [the longest x1 50.2 us: body(): pl.pallas_call(functools.partial(exchange, nchan), out_shape=(jax.ShapeDt...]
    all_gather x1 -> x0, waiting for transfers between devices: 37 us -> none  [body(): every_seg = lax.all_gather(white, 'tm', axis=0, tiled=True)]
    dot_general x4 -> x0, matrix products: 19.7 us -> none  [the longest x1 8.84 us: one_slot(): jnp.dot(cross.reshape(-1, 2 * nbins), itable, preferred_element_type=jnp....]
    dot_general x2 -> x0, local copies, waits for them, and re-layouts: 18.5 us -> none  [the longest x1 9.26 us: one_slot(): jnp.einsum('sif,sjf->ijf', left_pair, right_re, preferred_element_type=jn...]
    ppermute x2 -> x0, starting transfers between devices: 6.17 us -> none  [shifted(): return lax.ppermute(block, axis, route)]
    another operation x2 -> x1, other arithmetic: 6.77 us -> 0.61 us  [the longest x1 6.22 us: body(): window = jnp.stack([beside[1], every_seg, beside[-1]], axis=0)]
    psum x1 -> x0, blocking collectives: 5.69 us -> none  [body(): energy = lax.psum(jnp.sum(spectra * spectra, axis=(0, 2)), 'tm')]
  transfers between devices with their start and end apart: 3 -> 0, of which waited for: 3 -> 0; matrix products, arithmetic and copies ran while one was open for 0% -> 0% of each run, Pallas kernels for 0% -> 0%
where the time goes in v1:
time: 113 us; the launch traced here: 112 us
  Pallas kernels  99.8 us (88%)
  local copies, waits for them, and re-layouts  5.66 us (5%)
  between operations  4.32 us (4%)
  other arithmetic  2.34 us (2%)
    pallas_call x1, Pallas kernels, body(): pl.pallas_call(functools.partial(exchange, nchan), out_shape=(jax.ShapeDt...  50.2 us
    pallas_call x1, Pallas kernels, body(): pl.pallas_call(correlate, out_shape=jax.ShapeDtypeStruct((rows, block, LA...  49.6 us
    unnamed x6, local copies, waits for them, and re-layouts  4.12 us

profile of v1, /device:TPU:9, one launch (start us, length us, event | category | flops | bytes accessed | tf_op | source)
XLA Modules:
  0.0 112.2 jit_solution(13677211212833276235)
XLA Ops:
  0.7 1.3 %fusion.11 = (s32[1,1]{1,0:T(1,128)}, s32[1,1]{1,0:T(1,128)}) fusion(s32[1,2]{1,0:T(1,128)} %param.4), kind=kLoop, calls=%fused_computation.27 | loop fusion | bytes 16 | tf_op jit(solution)/shard_map/slice | solution.py:188
  5.6 0.1 add_convert_fusion
  5.7 0.1 broadcast_in_dim.8
  5.8 0.1 broadcast_in_dim.18
  5.8 0.1 broadcast_in_dim.19.flag_ref
  5.9 0.3 fusion.10
  6.3 0.6 fusion.3.inv_ref
  6.9 0.6 cosine_convert_fusion
  7.5 0.7 pad_maximum_fusion.fwd_ref
  8.2 0.0 copy-start.2
  8.2 1.2 %copy-done.2 = bf16[8,256,256]{2,1,0:T(8,128)(2,1)S(1)} copy-done((bf16[8,256,256]{2,1,0:T(8,128)(2,1)S(1)}, bf16[8,256,256]{2,1,0:T(8,128)(2,1)}, u32[]{:S(2)}) %copy-start.2) | copy-done | bytes 1048600
  9.4 50.2 %exchange.1 = (bf16[32,256,256]{2,1,0:T(8,128)(2,1)S(1)}, bf16[32,64,256]{2,1,0:T(8,128)(2,1)S(1)}) custom-call(bf16[8,256,256]{2,1,0:T(8,128)(2,1)S(1)} %copy-done.2, s32[24,256]{1,0:T(8,128)S(1)} %broadcast_in_dim.19.flag_ref), custom_call_target="tpu_custom_call" | custom-call | tf_op jit(solution)/shard_map/exchange/pallas_call | solution.py:195
  59.7 0.0 copy-start
  59.7 1.9 %copy-done = bf16[32,256,256]{2,1,0:T(8,128)(2,1)} copy-done((bf16[32,256,256]{2,1,0:T(8,128)(2,1)}, bf16[32,256,256]{2,1,0:T(8,128)(2,1)S(1)}, u32[]{:S(2)}) %copy-start) | copy-done | bytes 4194328
  61.6 0.0 copy-start.1
  61.6 1.0 copy-done.1
  62.6 49.6 %correlate.1 = bf16[64,256,128]{2,1,0:T(8,128)(2,1)} custom-call(s32[1]{0:T(128)S(6)} %copy.4.count_ref, bf16[32,256,256]{2,1,0:T(8,128)(2,1)} %copy-done, bf16[32,64,256]{2,1,0:T(8,128)(2,1)} %copy-done.1, bf16[256,256]{1,0:T(8,128)(2,1)} %pad_maximum_fusion.fwd_ref, bf16[128,256]{1,0:T(8,128)(2,1)} %fusion.3.inv_ref), custom_call_target="tpu_custom_call" | custom-call | tf_op jit(solution)/shard_map/correlate/pallas_call | solution.py:209
  (1 shorter events, 0.0 us)
Async XLA Ops:
  8.2 1.2 %copy-start.2 = (bf16[8,256,256]{2,1,0:T(8,128)(2,1)S(1)}, bf16[8,256,256]{2,1,0:T(8,128)(2,1)}, u32[]{:S(2)}) copy-start(bf16[8,256,256]{2,1,0:T(8,128)(2,1)} %x_ref.1) | copy-start | bytes 3145732
  59.7 1.9 %copy-start = (bf16[32,256,256]{2,1,0:T(8,128)(2,1)}, bf16[32,256,256]{2,1,0:T(8,128)(2,1)S(1)}, u32[]{:S(2)}) copy-start(bf16[32,256,256]{2,1,0:T(8,128)(2,1)S(1)} %get-tuple-element.7.r_ref) | copy-start | bytes 12582916
  61.6 1.0 copy-start.1

commit v2 on v1

v2 whole, which is shorter than its diff:
```python
import functools
import math

import jax
import jax.numpy as jnp
import numpy as np
from jax import lax
from jax.experimental import pallas as pl
from jax.experimental.pallas import tpu as pltpu
from jax.sharding import PartitionSpec as P

NF = 128
LAGS = 128
LANES = 128
PITCH = NF + 8
MESH = pl.DeviceIdType.MESH
F32 = jnp.float32
BF16 = jnp.bfloat16


def forward_table(samples, nbins):
    n_idx = np.arange(samples)[None, :]
    k_idx = np.arange(1, nbins + 1)[:, None]
    phase = (n_idx * k_idx % samples).astype(np.float32) * np.float32(2.0 * math.pi / samples)
    return jnp.asarray(np.concatenate([np.cos(phase), -np.sin(phase)], axis=0), BF16)


def inverse_table(samples, nbins, nlags):
    k_idx = np.arange(1, nbins + 1)[None, :]
    lag_idx = np.arange(nlags)[:, None] - nlags // 2
    phase = (k_idx * lag_idx % samples).astype(np.float32) * np.float32(2.0 * math.pi / samples)
    norm = np.float32(1.0 / math.sqrt(nbins))
    return jnp.asarray(np.concatenate([np.cos(phase), -np.sin(phase)], axis=1) * norm, BF16)


def pick(flag, yes, no):
    return jnp.where(flag > 0, yes.astype(F32), no.astype(F32)).astype(BF16)


def kernel(nchan, tile_ref, count_ref, x_ref, fwd_ref, inv_ref, o_ref,
           own, far, near, got, lsend, asked, wish, r_ref, l_ref, rspec, lspec, renergy, lenergy,
           cross, out, own_sem, a_send, a_recv, b_send, b_recv, w_send, w_recv,
           r_send, r_recv, l_send, l_recv, o_sem):
    segs, block, samples = own.shape
    nseg = r_ref.shape[0]
    rows = block // 4
    halves = block // LANES
    span = nseg * 2 * PITCH
    depth = NF * PITCH
    c = lax.axis_index("chan")
    t = lax.axis_index("tm")
    odd = lax.rem(c, 2)
    partner = c + 1 - 2 * odd
    z_to = lax.rem(c + nchan - 2 + 4 * odd, nchan)
    z_from = lax.rem(c + nchan + 2 - 4 * odd, nchan)
    core = lax.rem(t, 2)
    t1 = t + 1 - 2 * core
    t2 = lax.rem(t + 2, 4)
    t3 = lax.rem(t1 + 2, 4)

    mine = [pltpu.make_async_copy(x_ref.at[k], own.at[k], own_sem.at[k]) for k in range(segs)]
    for copy in mine:
        copy.start()
    row_b, col_b = tile_ref[0, 0], tile_ref[0, 1]
    beyond = jnp.where(odd == 1, jnp.maximum(row_b, col_b) - c, c - jnp.minimum(row_b, col_b))
    asked[...] = jnp.full(asked.shape, beyond, jnp.int32)
    take_r = jnp.full((1, samples), (col_b - c) * (col_b - c), jnp.int32)
    take_l = jnp.full((1, samples), (row_b - c) * (row_b - c), jnp.int32)
    renergy[...] = jnp.zeros_like(renergy)
    lenergy[...] = jnp.zeros_like(lenergy)

    barrier = pltpu.get_barrier_semaphore()
    for where in ((z_to, t), (z_from, t), (partner, t), (c, t1), (c, t2), (c, t3)):
        pl.semaphore_signal(barrier, inc=1, device_id=where, device_id_type=MESH)
    pl.semaphore_wait(barrier, 6)

    def send(src, dst, ss, rs, where):
        return pltpu.make_async_remote_copy(
            src_ref=src, dst_ref=dst, send_sem=ss, recv_sem=rs,
            device_id=where, device_id_type=MESH)

    ask = send(asked, wish, w_send, w_recv, (partner, t))
    ask.start()
    hop_a = [send(x_ref.at[k], far.at[k], a_send.at[k], a_recv.at[k], (z_to, t))
             for k in range(segs)]
    hop_b = [send(near.at[k], got.at[k], b_send.at[k], b_recv.at[k], (partner, t))
             for k in range(segs)]

    def share(k, slot, which, where):
        ref = r_ref.at[slot * segs + k]
        return send(ref, ref, r_send.at[which, k], r_recv.at[which, k], where)

    def share_l(k, which, peer):
        return send(lsend.at[k, pl.ds(pl.multiple_of(peer * rows, rows), rows)],
                    l_ref.at[t * segs + k],
                    l_send.at[which, k], l_recv.at[which, k], (c, peer))

    to_y = [share(k, t, 0, (c, t2)) for k in range(segs)]
    to_core = [share(k, t, 1, (c, t1)) for k in range(segs)]
    forward = [share(k, t2, 2, (c, t1)) for k in range(segs)]
    parts = [[share_l(k, w, p) for w, p in enumerate((t2, t3, t1))] for k in range(segs)]

    nt = (((1,), (1,)), ((), ()))
    lane = lax.broadcasted_iota(jnp.int32, (1, 2 * rows), 1)

    def spectra_r(s):
        spec = lax.dot_general(fwd_ref[...], r_ref[s], nt, preferred_element_type=F32)
        base = pl.multiple_of(s * 2 * PITCH, 8)
        for h in range(halves):
            cols = slice(h * LANES, (h + 1) * LANES)
            rspec[pl.ds(h * span + base, NF), :] = spec[:NF, cols]
            rspec[pl.ds(h * span + base + PITCH, NF), :] = spec[NF:, cols]
        renergy[...] += jnp.sum((spec * spec).reshape(2 * NF // 8, 8, block), axis=0)

    def spectra_l(s):
        left = l_ref[s]
        both = jnp.concatenate([left, left], axis=0)
        spec = lax.dot_general(fwd_ref[...], both, nt, preferred_element_type=F32)
        lenergy[...] += jnp.sum((spec * spec).reshape(2 * NF // 8, 8, 2 * rows), axis=0)
        base = pl.multiple_of(s * 2 * PITCH, 8)
        top, bottom = spec[:NF], spec[NF:]
        lspec[pl.ds(base, NF), :] = jnp.where(lane < rows, top, -bottom)
        lspec[pl.ds(base + PITCH, NF), :] = jnp.where(lane < rows, bottom, top)

    for k in range(segs):
        hop_a[k].start()
    ask.wait_recv()
    for step in range(segs + 4):
        k = step
        if k < segs:
            mine[k].wait()
            hop_a[k].wait_recv()
            near[k] = pick(wish[0:1, :], far[k], own[k])
            hop_b[k].start()
        k = step - 1
        if 0 <= k < segs:
            hop_b[k].wait_recv()
            r_ref[t * segs + k] = pick(take_r, got[k], own[k])
            to_y[k].start()
            lsend[k] = pick(take_l, got[k], own[k])
            for copy in parts[k]:
                copy.start()
            to_core[k].start()
            l_ref[t * segs + k] = lsend[k, pl.ds(pl.multiple_of(t * rows, rows), rows)]
            spectra_r(t * segs + k)
            spectra_l(t * segs + k)
        k = step - 3
        if 0 <= k < segs:
            to_y[k].wait_recv()
            forward[k].start()
            to_core[k].wait_recv()
            spectra_r(t1 * segs + k)
            parts[k][2].wait_recv()
            spectra_l(t1 * segs + k)
            spectra_r(t2 * segs + k)
        k = step - 4
        if 0 <= k < segs:
            parts[k][0].wait_recv()
            spectra_l(t2 * segs + k)
            parts[k][1].wait_recv()
            spectra_l(t3 * segs + k)
            forward[k].wait_recv()
            spectra_r(t3 * segs + k)
    ask.wait_send()
    for k in range(segs):
        hop_a[k].wait_send()
        hop_b[k].wait_send()
        to_y[k].wait_send()
        to_core[k].wait_send()
        forward[k].wait_send()
        for copy in parts[k]:
            copy.wait_send()

    count = count_ref[0]
    rscale = 1.0 / jnp.sqrt(jnp.sum(renergy[...], axis=0, keepdims=True) / (nseg * NF) + 1e-06)
    lscale = 1.0 / jnp.sqrt(jnp.sum(lenergy[...], axis=0, keepdims=True) / (nseg * NF) + 1e-06)
    seg_of = lax.broadcasted_iota(jnp.int32, (2 * nseg, 2 * rows), 0) // 2
    lscale = jnp.where(seg_of < count, jnp.broadcast_to(lscale, (2 * nseg, 2 * rows)), 0.0)

    def one_bin(f, _):
        right = jnp.concatenate(
            [rspec[pl.ds(h * span + f, 2 * nseg, stride=PITCH), :] for h in range(halves)], axis=1)
        right = (right * rscale).astype(BF16)
        left = (lspec[pl.ds(f, 2 * nseg, stride=PITCH), :] * lscale).astype(BF16)
        both = lax.dot_general(
            left, right, (((0,), (0,)), ((), ())), preferred_element_type=F32)
        base = pl.multiple_of(f * PITCH, 8)
        for h in range(halves):
            cross[pl.ds(h * depth + base, 2 * rows), :] = both[:, h * LANES:(h + 1) * LANES]
        return 0

    lax.fori_loop(0, NF, one_bin, 0, unroll=8)
    share = 1.0 / jnp.maximum(count, 1).astype(F32)

    def one_row(i, _):
        for h in range(halves):
            real = cross[pl.ds(h * depth + i, NF, stride=PITCH), :].astype(BF16)
            imag = cross[pl.ds(h * depth + rows + i, NF, stride=PITCH), :].astype(BF16)
            both = jnp.concatenate([real, imag], axis=0)
            corr = jnp.dot(inv_ref[...], both, preferred_element_type=F32) * share
            out[i, pl.ds(h * LANES, LANES), :] = corr.T.astype(BF16)
        return 0

    parts_out = 4
    piece = rows // parts_out
    copies = []
    for g in range(parts_out):
        lax.fori_loop(g * piece, (g + 1) * piece, one_row, 0, unroll=8)
        copy = pltpu.make_async_copy(out.at[pl.ds(g * piece, piece)],
                                     o_ref.at[pl.ds(g * piece, piece)], o_sem.at[g])
        copy.start()
        copies.append(copy)
    for copy in copies:
        copy.wait()


def body(nchan, traces, tile_list, seg_counts):
    segs, block, samples = traces.shape
    ntm = 4
    nseg = segs * ntm
    rows = block // ntm
    vmem = pl.BlockSpec(memory_space=pltpu.VMEM)
    smem = pl.BlockSpec(memory_space=pltpu.SMEM)
    hbm = pl.BlockSpec(memory_space=pl.ANY)
    dma = pltpu.SemaphoreType.DMA
    halves = block // LANES
    out = pl.pallas_call(
        functools.partial(kernel, nchan),
        out_shape=jax.ShapeDtypeStruct((rows, block, LAGS), BF16),
        in_specs=[smem, smem, hbm, vmem, vmem],
        out_specs=hbm,
        scratch_shapes=[pltpu.VMEM((segs, block, samples), BF16)] * 5 + [
            pltpu.VMEM((8, samples), jnp.int32), pltpu.VMEM((8, samples), jnp.int32),
            pltpu.VMEM((nseg, block, samples), BF16),
            pltpu.VMEM((nseg, rows, samples), BF16),
            pltpu.VMEM((halves * nseg * 2 * PITCH, LANES), F32),
            pltpu.VMEM((nseg * 2 * PITCH, 2 * rows), F32),
            pltpu.VMEM((8, block), F32), pltpu.VMEM((8, 2 * rows), F32),
            pltpu.VMEM((halves * NF * PITCH, LANES), F32),
            pltpu.VMEM((rows, block, LAGS), BF16),
            dma((segs,)), dma((segs,)), dma((segs,)), dma((segs,)), dma((segs,)), dma, dma,
            dma((3, segs)), dma((3, segs)), dma((3, segs)), dma((3, segs)), dma((4,))],
        compiler_params=pltpu.CompilerParams(
            collective_id=0, has_side_effects=True, vmem_limit_bytes=58 << 20),
        name="correlate",
    )(tile_list, seg_counts, traces, forward_table(samples, NF), inverse_table(samples, NF, LAGS))
    return out[None]


def solution(mesh):
    return jax.shard_map(
        functools.partial(body, mesh.shape["chan"]),
        mesh=mesh,
        in_specs=(P("tm", "chan", None), P("chan", None), P("chan")),
        out_specs=P("chan", "tm", None, None),
        check_vma=False,
    )
```

time: 113 us -> 71.2 us (0.63)
  Pallas kernels: 99.8 us -> 64.7 us
  between operations: 4.32 us -> 0.66 us
  other arithmetic: 2.34 us -> 0 us
    pallas_call x2 -> x1, Pallas kernels: 99.8 us -> 64.7 us  [body(): pl.pallas_call(functools.partial(kernel, nchan), out_shape=jax.ShapeDtype...]
    slice x1 -> x0, local copies, waits for them, and re-layouts: 1.31 us -> none  [body(): row_b, col_b = (tile_list[0, 0], tile_list[0, 1])]
    unnamed x6 -> x1, local copies, waits for them, and re-layouts: 4.12 us -> 4.7 us
where the time goes in v2:
time: 71.2 us; the launch traced here: 70.1 us
  Pallas kernels  64.7 us (91%)
  local copies, waits for them, and re-layouts  4.7 us (7%)
    pallas_call x1, Pallas kernels, body(): pl.pallas_call(functools.partial(kernel, nchan), out_shape=jax.ShapeDtype...  64.7 us
    unnamed x1, local copies, waits for them, and re-layouts  4.7 us

profile of v2, /device:TPU:9, one launch (start us, length us, event | category | flops | bytes accessed | tf_op | source)
XLA Modules:
  0.0 70.1 jit_solution(10575111390241549711)
XLA Ops:
  0.7 64.7 %correlate.1 = bf16[64,256,128]{2,1,0:T(8,128)(2,1)} custom-call(s32[1,2]{1,0:T(1,128)} %tile_ref.1, s32[1]{0:T(128)S(6)} %copy.7.count_ref, bf16[8,256,256]{2,1,0:T(8,128)(2,1)} %x_ref.1, bf16[256,256]{1,0:T(8,128)(2,1)} %constant.4.clone.fwd_ref, bf16[128,256]{1,0:T(8,128)(2,1)} %constant.5.clone.inv_ref), custom_call_target="tpu_custom_call" | custom-call | tf_op jit(solution)/shard_map/correlate/pallas_call | solution.py:227
  65.4 4.7 %copy.8 = bf16[1,64,256,128]{3,2,1,0:T(8,128)(2,1)} copy(bf16[1,64,256,128]{3,2,1,0:T(8,128)(2,1)} %bitcast.1) | data formatting | bytes 8388608

commit v3 on v2

v3 whole, which is shorter than its diff:
```python
import functools
import math

import jax
import jax.numpy as jnp
import numpy as np
from jax import lax
from jax.experimental import pallas as pl
from jax.experimental.pallas import tpu as pltpu
from jax.sharding import PartitionSpec as P

NF = 128
LAGS = 128
LANES = 128
PITCH = NF + 8
OUT_PITCH = NF + 4
LIMIT = 40
MESH = pl.DeviceIdType.MESH
F32 = jnp.float32
BF16 = jnp.bfloat16


def forward_table(samples, nbins):
    n_idx = np.arange(samples)[None, :]
    k_idx = np.arange(1, nbins + 1)[:, None]
    phase = (n_idx * k_idx % samples).astype(np.float32) * np.float32(2.0 * math.pi / samples)
    return jnp.asarray(np.concatenate([np.cos(phase), -np.sin(phase)], axis=0), BF16)


def inverse_table(samples, nbins, nlags):
    k_idx = np.arange(1, nbins + 1)[None, :]
    lag_idx = np.arange(nlags)[:, None] - nlags // 2
    phase = (k_idx * lag_idx % samples).astype(np.float32) * np.float32(2.0 * math.pi / samples)
    norm = np.float32(1.0 / math.sqrt(nbins))
    return jnp.asarray(np.concatenate([np.cos(phase), -np.sin(phase)], axis=1) * norm, BF16)


def pick(flag, yes, no):
    return jnp.where(flag > 0, yes.astype(F32), no.astype(F32)).astype(BF16)


def kernel(nchan, tile_ref, count_ref, x_ref, fwd_ref, inv_ref, o_ref,
           own, far, near, got, lsend, asked, wish, r_ref, l_ref, rspec, lspec, renergy, lenergy,
           cross, own_sem, a_send, a_recv, b_send, b_recv, w_send, w_recv,
           r_send, r_recv, l_send, l_recv):
    segs, block, samples = own.shape
    nseg = r_ref.shape[0]
    rows = block // 4
    halves = block // LANES
    span = nseg * 2 * PITCH
    c = lax.axis_index("chan")
    t = lax.axis_index("tm")
    odd = lax.rem(c, 2)
    partner = c + 1 - 2 * odd
    z_to = lax.rem(c + nchan - 2 + 4 * odd, nchan)
    z_from = lax.rem(c + nchan + 2 - 4 * odd, nchan)
    core = lax.rem(t, 2)
    t1 = t + 1 - 2 * core
    t2 = lax.rem(t + 2, 4)
    t3 = lax.rem(t1 + 2, 4)

    mine = [pltpu.make_async_copy(x_ref.at[k], own.at[k], own_sem.at[k]) for k in range(segs)]
    for copy in mine:
        copy.start()
    row_b, col_b = tile_ref[0, 0], tile_ref[0, 1]
    beyond = jnp.where(odd == 1, jnp.maximum(row_b, col_b) - c, c - jnp.minimum(row_b, col_b))
    asked[...] = jnp.full(asked.shape, beyond, jnp.int32)
    take_r = jnp.full((1, samples), (col_b - c) * (col_b - c), jnp.int32)
    take_l = jnp.full((1, samples), (row_b - c) * (row_b - c), jnp.int32)
    renergy[...] = jnp.zeros_like(renergy)
    lenergy[...] = jnp.zeros_like(lenergy)

    barrier = pltpu.get_barrier_semaphore()
    for where in ((z_to, t), (z_from, t), (partner, t), (c, t1), (c, t2), (c, t3)):
        pl.semaphore_signal(barrier, inc=1, device_id=where, device_id_type=MESH)
    pl.semaphore_wait(barrier, 6)

    def send(src, dst, ss, rs, where):
        return pltpu.make_async_remote_copy(
            src_ref=src, dst_ref=dst, send_sem=ss, recv_sem=rs,
            device_id=where, device_id_type=MESH)

    ask = send(asked, wish, w_send, w_recv, (partner, t))
    ask.start()
    hop_a = [send(x_ref.at[k], far.at[k], a_send.at[k], a_recv.at[k], (z_to, t))
             for k in range(segs)]
    hop_b = [send(near.at[k], got.at[k], b_send.at[k], b_recv.at[k], (partner, t))
             for k in range(segs)]

    def share(k, h, slot, which, where):
        ref = r_ref.at[slot * segs + k, pl.ds(h * LANES, LANES)]
        return send(ref, ref, r_send.at[which, h, k], r_recv.at[which, h, k], where)

    def share_l(k, which, peer):
        return send(lsend.at[k, pl.ds(pl.multiple_of(peer * rows, rows), rows)],
                    l_ref.at[t * segs + k],
                    l_send.at[which, k], l_recv.at[which, k], (c, peer))

    to_y = [[share(k, h, t, 0, (c, t2)) for k in range(segs)] for h in range(halves)]
    to_core = [[share(k, h, t, 1, (c, t1)) for k in range(segs)] for h in range(halves)]
    forward = [[share(k, h, t2, 2, (c, t1)) for k in range(segs)] for h in range(halves)]
    parts = [[share_l(k, w, p) for w, p in enumerate((t2, t3, t1))] for k in range(segs)]

    nt = (((1,), (1,)), ((), ()))
    lane = lax.broadcasted_iota(jnp.int32, (1, 2 * rows), 1)

    def spectra_r(s, h):
        spec = lax.dot_general(fwd_ref[...], r_ref[s, pl.ds(h * LANES, LANES)], nt,
                               preferred_element_type=F32)
        base = pl.multiple_of(h * span + s * 2 * PITCH, 8)
        rspec[pl.ds(base, NF), :] = spec[:NF]
        rspec[pl.ds(base + PITCH, NF), :] = spec[NF:]
        renergy[h] += jnp.sum((spec * spec).reshape(2 * NF // 8, 8, LANES), axis=0)

    def spectra_l(s):
        left = l_ref[s]
        both = jnp.concatenate([left, left], axis=0)
        spec = lax.dot_general(fwd_ref[...], both, nt, preferred_element_type=F32)
        lenergy[...] += jnp.sum((spec * spec).reshape(2 * NF // 8, 8, 2 * rows), axis=0)
        base = pl.multiple_of(s * 2 * PITCH, 8)
        top, bottom = spec[:NF], spec[NF:]
        lspec[pl.ds(base, NF), :] = jnp.where(lane < rows, top, -bottom)
        lspec[pl.ds(base + PITCH, NF), :] = jnp.where(lane < rows, bottom, top)

    for k in range(segs):
        hop_a[k].start()
    ask.wait_recv()
    for step in range(segs + 4):
        k = step
        if k < segs:
            mine[k].wait()
            hop_a[k].wait_recv()
            near[k] = pick(wish[0:1, :], far[k], own[k])
            hop_b[k].start()
        k = step - 1
        if 0 <= k < segs:
            hop_b[k].wait_recv()
            r_ref[t * segs + k] = pick(take_r, got[k], own[k])
            to_y[0][k].start()
            lsend[k] = pick(take_l, got[k], own[k])
            for copy in parts[k]:
                copy.start()
            to_core[0][k].start()
            l_ref[t * segs + k] = lsend[k, pl.ds(pl.multiple_of(t * rows, rows), rows)]
            if k == segs - 1:
                for h in range(1, halves):
                    for i in range(segs):
                        to_y[h][i].start()
                        to_core[h][i].start()
            spectra_r(t * segs + k, 0)
            spectra_l(t * segs + k)
        k = step - 3
        if 0 <= k < segs:
            to_y[0][k].wait_recv()
            forward[0][k].start()
            to_core[0][k].wait_recv()
            spectra_r(t1 * segs + k, 0)
            parts[k][2].wait_recv()
            spectra_l(t1 * segs + k)
            spectra_r(t2 * segs + k, 0)
        k = step - 4
        if 0 <= k < segs:
            parts[k][0].wait_recv()
            spectra_l(t2 * segs + k)
            parts[k][1].wait_recv()
            spectra_l(t3 * segs + k)
            forward[0][k].wait_recv()
            spectra_r(t3 * segs + k, 0)

    count = count_ref[0]
    lscale = 1.0 / jnp.sqrt(jnp.sum(lenergy[...], axis=0, keepdims=True) / (nseg * NF) + 1e-06)
    seg_of = lax.broadcasted_iota(jnp.int32, (2 * nseg, 2 * rows), 0) // 2
    lscale = jnp.where(seg_of < count, jnp.broadcast_to(lscale, (2 * nseg, 2 * rows)), 0.0)
    share_n = 1.0 / jnp.maximum(count, 1).astype(F32)

    def stack(h):
        rscale = jnp.sum(renergy[h], axis=0, keepdims=True) / (nseg * NF) + 1e-06
        rscale = 1.0 / jnp.sqrt(rscale)

        def one_bin(f, _):
            right = rspec[pl.ds(h * span + f, 2 * nseg, stride=PITCH), :]
            right = (right * rscale).astype(BF16)
            left = (lspec[pl.ds(f, 2 * nseg, stride=PITCH), :] * lscale).astype(BF16)
            cross[pl.ds(f * OUT_PITCH, 2 * rows), :] = lax.dot_general(
                left, right, (((0,), (0,)), ((), ())), preferred_element_type=F32)
            return 0

        lax.fori_loop(0, NF, one_bin, 0, unroll=16)

    def lags(h, first, last):
        def one_row(i, _):
            real = cross[pl.ds(i, NF, stride=OUT_PITCH), :].astype(BF16)
            imag = cross[pl.ds(rows + i, NF, stride=OUT_PITCH), :].astype(BF16)
            both = jnp.concatenate([real, imag], axis=0)
            corr = jnp.dot(inv_ref[...], both, preferred_element_type=F32) * share_n
            o_ref[i, pl.ds(h * LANES, LANES), :] = corr.T.astype(BF16)
            return 0

        lax.fori_loop(first, last, one_row, 0, unroll=16)

    stack(0)
    for h in range(1, halves):
        for k in range(segs // 2):
            to_y[h][k].wait_recv()
            forward[h][k].start()
        lags(h - 1, 0, rows)
        for k in range(segs // 2, segs):
            to_y[h][k].wait_recv()
            forward[h][k].start()
            spectra_r(t * segs + k, h)
            spectra_r(t * segs + k - segs // 2, h)
            to_core[h][k].wait_recv()
            to_core[h][k - segs // 2].wait_recv()
            spectra_r(t1 * segs + k, h)
            spectra_r(t1 * segs + k - segs // 2, h)
            spectra_r(t2 * segs + k - segs // 2, h)
            forward[h][k - segs // 2].wait_recv()
            spectra_r(t3 * segs + k - segs // 2, h)
        for k in range(segs // 2, segs):
            spectra_r(t2 * segs + k, h)
            forward[h][k].wait_recv()
            spectra_r(t3 * segs + k, h)
        stack(h)
    lags(halves - 1, 0, rows)

    ask.wait_send()
    for k in range(segs):
        hop_a[k].wait_send()
        hop_b[k].wait_send()
        for h in range(halves):
            to_y[h][k].wait_send()
            to_core[h][k].wait_send()
            forward[h][k].wait_send()
        for copy in parts[k]:
            copy.wait_send()


def body(nchan, traces, tile_list, seg_counts):
    segs, block, samples = traces.shape
    ntm = 4
    nseg = segs * ntm
    rows = block // ntm
    vmem = pl.BlockSpec(memory_space=pltpu.VMEM)
    smem = pl.BlockSpec(memory_space=pltpu.SMEM)
    hbm = pl.BlockSpec(memory_space=pltpu.HBM)
    dma = pltpu.SemaphoreType.DMA
    halves = block // LANES
    out = pl.pallas_call(
        functools.partial(kernel, nchan),
        out_shape=jax.ShapeDtypeStruct((rows, block, LAGS), BF16),
        in_specs=[smem, smem, hbm, vmem, vmem],
        out_specs=vmem,
        scratch_shapes=[pltpu.VMEM((segs, block, samples), BF16)] * 5 + [
            pltpu.VMEM((8, samples), jnp.int32), pltpu.VMEM((8, samples), jnp.int32),
            pltpu.VMEM((nseg, block, samples), BF16),
            pltpu.VMEM((nseg, rows, samples), BF16),
            pltpu.VMEM((halves * nseg * 2 * PITCH, LANES), F32),
            pltpu.VMEM((nseg * 2 * PITCH, 2 * rows), F32),
            pltpu.VMEM((halves, 8, LANES), F32), pltpu.VMEM((8, 2 * rows), F32),
            pltpu.VMEM((NF * OUT_PITCH, LANES), F32),
            dma((segs,)), dma((segs,)), dma((segs,)), dma((segs,)), dma((segs,)), dma, dma,
            dma((3, halves, segs)), dma((3, halves, segs)), dma((3, segs)), dma((3, segs))],
        compiler_params=pltpu.CompilerParams(
            collective_id=0, has_side_effects=True, vmem_limit_bytes=LIMIT << 20),
        name="correlate",
    )(tile_list, seg_counts, traces, forward_table(samples, NF), inverse_table(samples, NF, LAGS))
    return out[None]


def solution(mesh):
    return jax.shard_map(
        functools.partial(body, mesh.shape["chan"]),
        mesh=mesh,
        in_specs=(P("tm", "chan", None), P("chan", None), P("chan")),
        out_specs=P("chan", "tm", None, None),
        check_vma=False,
    )
```

time: 71.2 us -> 67.7 us (0.951); the launches traced: 70.1 us -> 67.3 us
  Pallas kernels: 64.7 us -> 61 us
  local copies, waits for them, and re-layouts: 4.7 us -> 5.63 us
    pallas_call x1, Pallas kernels: 64.7 us -> 61 us  [body(): pl.pallas_call(functools.partial(kernel, nchan), out_shape=jax.ShapeDtype...]
    unnamed x1 -> x9, local copies, waits for them, and re-layouts: 4.7 us -> 5.63 us
where the time goes in v3:
time: 67.7 us; the launch traced here: 67.3 us
  Pallas kernels  61 us (90%)
  local copies, waits for them, and re-layouts  5.63 us (8%)
    pallas_call x1, Pallas kernels, body(): pl.pallas_call(functools.partial(kernel, nchan), out_shape=jax.ShapeDtype...  61 us
    unnamed x9, local copies, waits for them, and re-layouts  5.63 us

profile of v3, /device:TPU:9, one launch (start us, length us, event | category | flops | bytes accessed | tf_op | source)
XLA Modules:
  0.0 67.3 jit_solution(9066093148439625120)
XLA Ops:
  0.7 0.0 copy-start
  0.7 1.2 %copy-done = bf16[8,256,256]{2,1,0:T(8,128)(2,1)S(1)} copy-done((bf16[8,256,256]{2,1,0:T(8,128)(2,1)S(1)}, bf16[8,256,256]{2,1,0:T(8,128)(2,1)}, u32[]{:S(2)}) %copy-start) | copy-done | bytes 1048600
  1.9 0.0 copy-start.1
  1.9 0.9 %copy-done.1 = bf16[256,256]{1,0:T(8,128)(2,1)S(1)} copy-done((bf16[256,256]{1,0:T(8,128)(2,1)S(1)}, bf16[256,256]{1,0:T(8,128)(2,1)}, u32[]{:S(2)}) %copy-start.1) | copy-done | bytes 131096
  2.8 0.0 copy-start.2
  2.8 0.8 %copy-done.2 = bf16[128,256]{1,0:T(8,128)(2,1)S(1)} copy-done((bf16[128,256]{1,0:T(8,128)(2,1)S(1)}, bf16[128,256]{1,0:T(8,128)(2,1)}, u32[]{:S(2)}) %copy-start.2) | copy-done | bytes 65560
  3.6 0.0 copy-start.3
  3.6 0.7 copy-done.3
  4.3 61.0 %correlate.1 = bf16[64,256,128]{2,1,0:T(8,128)(2,1)S(1)} custom-call(s32[1,2]{1,0:T(1,128)S(1)} %copy-done.3, s32[1]{0:T(128)S(6)} %copy.7.count_ref, bf16[8,256,256]{2,1,0:T(8,128)(2,1)S(1)} %copy-done, bf16[256,256]{1,0:T(8,128)(2,1)S(1)} %copy-done.1, bf16[128,256]{1,0:T(8,128)(2,1)S(1)} %copy-done.2), custom_call_target="tpu_custom_call" | custom-call | tf_op jit(solution)/shard_map/correlate/pallas_call | solution.py:248
  65.3 2.0 %copy.8 = bf16[1,64,256,128]{3,2,1,0:T(8,128)(2,1)} copy(bf16[1,64,256,128]{3,2,1,0:T(8,128)(2,1)S(1)} %bitcast.1) | data formatting | bytes 8388608
Async XLA Ops:
  0.7 1.2 %copy-start = (bf16[8,256,256]{2,1,0:T(8,128)(2,1)S(1)}, bf16[8,256,256]{2,1,0:T(8,128)(2,1)}, u32[]{:S(2)}) copy-start(bf16[8,256,256]{2,1,0:T(8,128)(2,1)} %x_ref.1) | copy-start | bytes 3145732
  1.9 0.9 %copy-start.1 = (bf16[256,256]{1,0:T(8,128)(2,1)S(1)}, bf16[256,256]{1,0:T(8,128)(2,1)}, u32[]{:S(2)}) copy-start(bf16[256,256]{1,0:T(8,128)(2,1)} %constant.4.clone.fwd_ref) | copy-start | bytes 393220
  2.8 0.8 %copy-start.2 = (bf16[128,256]{1,0:T(8,128)(2,1)S(1)}, bf16[128,256]{1,0:T(8,128)(2,1)}, u32[]{:S(2)}) copy-start(bf16[128,256]{1,0:T(8,128)(2,1)} %constant.5.clone.inv_ref) | copy-start | bytes 196612
  3.6 0.7 copy-start.3
